TPU v7x, 32 devices: a whole 2x2x4 slice. The times are simulated.
32 devices in a mesh: groups: 1, expert: 4 (over z), tensor: 4 (over y, x), seq: 2 (over core).
Axes of the slice: x: 2, y: 2, z: 4, core: 2. Of those that a mesh axis runs over, the one named last changes fastest.
Arguments:
- tokens: bfloat16 [2048, 2048], P(('groups', 'expert', 'seq'), 'tensor'), may hold values from -6 to 6
- expert_ids: int32 [2048, 8], P(('groups', 'expert', 'seq')), may hold values from 0 to 15, all different within a row; in each aligned block of 256 rows (0 to 255, 256 to 511, ...) at most 256 rows name the same one
- router_scores: float32 [2048, 8], P(('groups', 'expert', 'seq')), may hold values from 0.05 to 1
- w_gate: bfloat16 [16, 2048, 768], P(('expert', 'tensor'), None, 'seq'), may hold values from -0.125 to 0.125
- w_up: bfloat16 [16, 2048, 768], P(('expert', 'tensor'), None, 'seq'), may hold values from -0.125 to 0.125
- w_down: bfloat16 [16, 768, 2048], P(('expert', 'tensor'), 'seq'), may hold values from -0.21875 to 0.21875
Outputs:
- mixed: bfloat16 [2048, 2048], P(('groups', 'expert', 'seq'), 'tensor')
Inputs may be any that keep to these rules, and one draw needn't show every extreme that they name: `expert_ids`: each row names 8 different experts. In each aligned block of 256 rows (the rows of one device) no expert is named by more than 256 rows, a bound that some block reaches.
All inputs are finite; a program needn't handle non-finite values.
Results may differ from a plain program's by a relative error of at most 0.0061.
Values may be sent and summed in bfloat16 or wider, within the bound.
A program may use at most 64 MiB of HBM per device.

v0:
```python
import jax
import jax.numpy as jnp
from jax import lax
from jax.sharding import PartitionSpec as P


def from_partner(value, axis, distance):
    mask = 2**distance
    pairs = [(source, source ^ mask) for source in range(lax.axis_size(axis))]
    return lax.ppermute(value, axis, pairs)


def expert_partial(block, gate_w, up_w, down_w):
    gate = jnp.einsum("...ecd,edf->...ecf", block, gate_w, preferred_element_type=jnp.float32)
    upper = jnp.einsum("...ecd,edf->...ecf", block, up_w, preferred_element_type=jnp.float32)
    hidden = (jax.nn.silu(gate) * upper).astype(jnp.bfloat16)
    return jnp.einsum("...ecf,efd->...ecd", hidden, down_w, preferred_element_type=jnp.float32)


def round_half(values):
    kept = lax.optimization_barrier(values.astype(jnp.bfloat16))
    return kept.astype(jnp.float32)


def slot_positions(keys, count):
    onehot = (keys[:, None] == jnp.arange(count, dtype=jnp.int32)[None, :]).astype(jnp.int32)
    before = jnp.cumsum(onehot, axis=0) - onehot
    return jnp.sum(before * onehot, axis=1)


def body(tokens, expert_ids, router_scores, w_gate, w_up, w_down):
    tok_rows, top = expert_ids.shape
    exp_dev = w_gate.shape[0]
    n_owner = lax.axis_size("expert")
    n_tensor = lax.axis_size("tensor")
    experts_all = exp_dev * n_owner * n_tensor
    slots = min(tok_rows, max(2, tok_rows * top * 2 // experts_all))
    buckets = n_owner * exp_dev
    shares = router_scores / jnp.sum(router_scores, axis=1, keepdims=True)
    flat_ids = expert_ids.reshape(-1)
    source_row = jnp.arange(tok_rows * top, dtype=jnp.int32) // top
    whole = lax.all_gather(tokens, "tensor", axis=1, tiled=True)
    column = lax.axis_index("tensor")
    mine = flat_ids // exp_dev % n_tensor == column
    bucket = flat_ids // (exp_dev * n_tensor) * exp_dev + flat_ids % exp_dev
    masked = jnp.where(mine, bucket, buckets)
    position = slot_positions(masked, buckets)
    target = jnp.where(mine, bucket * slots + position, buckets * slots)
    width = whole.shape[1]
    outgoing = (
        jnp.zeros((buckets * slots + 1, width), jnp.bfloat16).at[target].set(whole[source_row])
    )
    outgoing = outgoing[: buckets * slots].reshape(n_owner, exp_dev, slots, width)
    arrived = lax.all_to_all(outgoing, "expert", split_axis=0, concat_axis=0, tiled=True)
    other_gate, other_up, other_down = from_partner((w_gate, w_up, w_down), "seq", 0)
    own_part = expert_partial(arrived, w_gate, w_up, w_down)
    far_part = expert_partial(arrived, other_gate, other_up, other_down)
    answer = (own_part + round_half(far_part)).astype(jnp.bfloat16)
    back = lax.all_to_all(answer, "expert", split_axis=0, concat_axis=0, tiled=True)
    width = back.shape[-1]
    flat_back = jnp.concatenate(
        [back.reshape(buckets * slots, width), jnp.zeros((1, width), jnp.bfloat16)], axis=0
    )
    picked = flat_back[target].reshape(tok_rows, top, width)
    share_mine = jnp.where(mine.reshape(tok_rows, top), shares, 0.0)
    combined = jnp.sum(picked.astype(jnp.float32) * share_mine[:, :, None], axis=1)
    return lax.psum_scatter(combined, "tensor", scatter_dimension=1, tiled=True).astype(
        jnp.bfloat16
    )


def solution(mesh):
    placed = (
        P(("groups", "expert", "seq"), "tensor"),
        P(("groups", "expert", "seq"), None),
        P(("groups", "expert", "seq"), None),
        P(("expert", "tensor"), None, "seq"),
        P(("expert", "tensor"), None, "seq"),
        P(("expert", "tensor"), "seq", None),
    )
    return jax.shard_map(
        body,
        mesh=mesh,
        in_specs=placed,
        out_specs=P(("groups", "expert", "seq"), "tensor"),
        check_vma=False,
    )
```

profile of v0, /device:TPU:0, one launch (start us, length us, event | category | flops | bytes accessed | tf_op | source)
XLA Modules:
  0.0 401.0 jit_solution(18035733251140253994)
XLA Ops:
  6.5 0.7 all-gather.2.cloned.1.call-update
  7.3 0.8 copy.12
  8.5 1.2 reduce-window.6
  9.6 0.2 slice_reduce_fusion
  10.3 28.1 %all-gather.2.cloned.1.call-done = bf16[256,2048]{1,0:T(8,128)(2,1)} async-done(((bf16[256,512]{1,0:T(8,128)(2,1)}), bf16[256,2048]{1,0:T(8,128)(2,1)}) %all-gather.2.cloned.1.call-update) | async-done | bytes 1048592 | tf_op jit(solution)/shard_map/all_gather | solution.py:42
  38.4 41.8 %scatter_custom_fusion = bf16[1025,2048]{1,0:T(8,128)(2,1)} fusion(s32[2048]{0:T(1024)S(1)} %bitcast.170, bf16[256,2048]{1,0:T(8,128)(2,1)} %all-gather.2.cloned.1.call-done, s32[2048]{0:T(1024)S(1)} %broadcast_clamp_fusion.1, bf16[]{:T(256)} %constant.75.clone.1), kind=kCustom, calls=%fused_computation.7 | custom fusion | bytes 4198912 | tf_op jit(solution)/shard_map/scatter | solution.py:51
  80.2 4.7 %slice.17 = bf16[1024,2048]{1,0:T(8,128)(2,1)} slice(bf16[1025,2048]{1,0:T(8,128)(2,1)} %scatter_custom_fusion), slice={[0:1024], [0:2048]} | slice | bytes 8388608 | tf_op jit(solution)/shard_map/slice | solution.py:53
  85.0 5.4 %all-to-all-start = ((bf16[4,1,256,2048]{3,2,1,0:T(8,128)(2,1)}), bf16[4,1,256,2048]{3,2,1,0:T(8,128)(2,1)}, u32[]{:S(2)}, u32[]{:S(2)}) async-start(bf16[4,1,256,2048]{3,2,1,0:T(8,128)(2,1)} %bitcast.169), calls=%async_computation | async-start | bytes 8388608 | tf_op jit(solution)/shard_map/all_to_all | solution.py:54
  90.5 0.5 collective-permute-start.2
  91.0 4.5 %collective-permute-done.1 = bf16[1,2048,384]{2,1,0:T(8,128)(2,1)} collective-permute-done((bf16[1,2048,384]{2,1,0:T(8,128)(2,1)}, bf16[1,2048,384]{2,1,0:T(8,128)(2,1)}, u32[]{:S(2)}, u32[]{:S(2)}) %collective-permute-start.1) | collective-permute-done | bytes 1572896 | tf_op jit(solution)/shard_map/ppermute | solution.py:10
  95.5 88.2 %all-to-all-done = bf16[4,1,256,2048]{3,2,1,0:T(8,128)(2,1)} async-done(((bf16[4,1,256,2048]{3,2,1,0:T(8,128)(2,1)}), bf16[4,1,256,2048]{3,2,1,0:T(8,128)(2,1)}, u32[]{:S(2)}, u32[]{:S(2)}) %all-to-all-start) | async-done | bytes 4194336 | tf_op jit(solution)/shard_map/all_to_all | solution.py:54
  183.7 6.2 %fusion.5 = f32[4,256,384]{2,1,0:T(8,128)} fusion(bf16[4,1,256,2048]{3,2,1,0:T(8,128)(2,1)} %all-to-all-done, bf16[1,2048,384]{2,1,0:T(8,128)(2,1)} %collective-permute-done.1), kind=kOutput, calls=%fused_computation.10 | convolution fusion | flops 1610612736 | bytes 7340032 | tf_op jit(solution)/shard_map/...ecd,edf->...ecf/dot_general | solution.py:15
  189.8 10.0 %convert_bitcast_fusion = bf16[4,1,256,2048]{3,2,0,1:T(8,128)(2,1)} fusion(bf16[1,384,2048]{2,1,0:T(8,128)(2,1)} %collective-permute-done.2, f32[4,256,384]{2,1,0:T(8,128)} %fusion.5, bf16[4,1,256,2048]{3,2,1,0:T(8,128)(2,1)} %all-to-all-done, bf16[1,2048,384]{2,1,0:T(8,128)(2,1)} %collective-permute-done), kind=kOutput, calls=%fused_computation.18 | convolution fusion | flops 3225681920 | bytes 13107200 | tf_op jit(solution)/shard_map/...ecf,efd->...ecd/dot_general | solution.py:17
  199.9 5.7 %fusion.11 = f32[4,256,384]{2,1,0:T(8,128)} fusion(bf16[4,1,256,2048]{3,2,1,0:T(8,128)(2,1)} %all-to-all-done, bf16[1,2048,384]{2,1,0:T(8,128)(2,1)S(1)} %copy-done.2), kind=kOutput, calls=%fused_computation.16 | convolution fusion | flops 1610612736 | bytes 7340032 | tf_op jit(solution)/shard_map/...ecd,edf->...ecf/dot_general | solution.py:14
  205.6 10.9 %fusion.22 = f32[4,256,2048]{2,1,0:T(8,128)} fusion(bf16[1,384,2048]{2,1,0:T(8,128)(2,1)S(1)} %copy-done.3, bf16[1,2048,384]{2,1,0:T(8,128)(2,1)} %param.10, bf16[4,1,256,2048]{3,2,1,0:T(8,128)(2,1)} %all-to-all-done, f32[4,256,384]{2,1,0:T(8,128)} %fusion.11), kind=kOutput, calls=%fused_computation.32 | convolution fusion | flops 3223584768 | bytes 17301504 | tf_op jit(solution)/shard_map/...ecf,efd->...ecd/dot_general | solution.py:17
  216.4 8.3 %fusion.4 = bf16[4,1,256,2048]{3,2,1,0:T(8,128)(2,1)} fusion(bf16[4,1,256,2048]{3,2,0,1:T(8,128)(2,1)} %convert_bitcast_fusion, f32[4,256,2048]{2,1,0:T(8,128)} %fusion.22), kind=kLoop, calls=%fused_computation.9 | loop fusion | flops 6291456 | bytes 16777216 | tf_op jit(solution)/shard_map/convert_element_type | solution.py:58
  224.7 5.0 %all-to-all-start.1 = ((bf16[4,1,256,2048]{3,2,1,0:T(8,128)(2,1)}), bf16[4,1,256,2048]{3,2,1,0:T(8,128)(2,1)}, u32[]{:S(2)}, u32[]{:S(2)}) async-start(bf16[4,1,256,2048]{3,2,1,0:T(8,128)(2,1)} %fusion.4), calls=%async_computation.1 | async-start | bytes 8388608 | tf_op jit(solution)/shard_map/all_to_all | solution.py:59
  229.7 0.3 reduce-scatter.2.cloned.1.call-start
  230.2 92.3 %all-to-all-done.1 = bf16[4,1,256,2048]{3,2,1,0:T(8,128)(2,1)} async-done(((bf16[4,1,256,2048]{3,2,1,0:T(8,128)(2,1)}), bf16[4,1,256,2048]{3,2,1,0:T(8,128)(2,1)}, u32[]{:S(2)}, u32[]{:S(2)}) %all-to-all-start.1) | async-done | bytes 4194336 | tf_op jit(solution)/shard_map/all_to_all | solution.py:59
  322.5 4.8 %concatenate.3 = bf16[1025,2048]{1,0:T(8,128)(2,1)} pad(bf16[1024,2048]{1,0:T(8,128)(2,1)} %bitcast.43, bf16[]{:T(256)} %constant.75.clone.1), padding=0_1x0_0 | pad | bytes 8392706 | tf_op jit(solution)/shard_map/concatenate | solution.py:61
  327.2 19.1 %gather_fusion = bf16[2048,2048]{1,0:T(8,128)(2,1)} fusion(bf16[1025,2048]{1,0:T(8,128)(2,1)} %concatenate.3, s32[2048]{0:T(1024)S(1)} %broadcast_clamp_fusion), kind=kCustom, calls=%fused_computation.1 | custom fusion | bytes 16785408 | tf_op jit(solution)/shard_map/gather | solution.py:64
  346.3 12.6 %fusion = f32[256,2048]{1,0:T(8,128)} fusion(bf16[2048,2048]{1,0:T(8,128)(2,1)} %gather_fusion, f32[256,8]{1,0:T(8,128)S(1)} %copy.16), kind=kLoop, calls=%fused_computation.4 | loop fusion | flops 12058624 | bytes 10493952 | tf_op jit(solution)/shard_map/reduce_sum | solution.py:66
  358.9 33.5 %reduce-scatter.2.cloned.1.call-done = f32[256,512]{1,0:T(8,128)} async-done(((f32[256,2048]{1,0:T(8,128)}), f32[256,512]{1,0:T(8,128)}) %reduce-scatter.2.cloned.1.call-update) | async-done | bytes 524304 | tf_op jit(solution)/shard_map/reduce_scatter | solution.py:67
  392.3 1.8 convert_element_type.52
  (30 shorter events, 1.1 us)
Async XLA Ops:
  6.5 31.9 %all-gather.2.cloned.1.call-start = ((), (), s32[]{:S(2)}) async-start(), calls=%async_computation.3 | async-start | bytes 1310720 | tf_op jit(solution)/shard_map/all_gather | solution.py:42
  85.0 5.5 %copy-start.3 = (bf16[1,384,2048]{2,1,0:T(8,128)(2,1)S(1)}, bf16[1,384,2048]{2,1,0:T(8,128)(2,1)}, u32[]{:S(2)}) copy-start(bf16[1,384,2048]{2,1,0:T(8,128)(2,1)} %param.11) | copy-start | bytes 4718596
  85.0 6.0 %copy-start.2 = (bf16[1,2048,384]{2,1,0:T(8,128)(2,1)S(1)}, bf16[1,2048,384]{2,1,0:T(8,128)(2,1)}, u32[]{:S(2)}) copy-start(bf16[1,2048,384]{2,1,0:T(8,128)(2,1)} %param.9) | copy-start | bytes 4718596
  85.0 98.7 %all-to-all-start = ((bf16[4,1,256,2048]{3,2,1,0:T(8,128)(2,1)}), bf16[4,1,256,2048]{3,2,1,0:T(8,128)(2,1)}, u32[]{:S(2)}, u32[]{:S(2)}) async-start(bf16[4,1,256,2048]{3,2,1,0:T(8,128)(2,1)} %bitcast.169), calls=%async_computation | async-start | bytes 8388608 | tf_op jit(solution)/shard_map/all_to_all | solution.py:54
  90.4 5.1 %collective-permute-start.1 = (bf16[1,2048,384]{2,1,0:T(8,128)(2,1)}, bf16[1,2048,384]{2,1,0:T(8,128)(2,1)}, u32[]{:S(2)}, u32[]{:S(2)}) collective-permute-start(bf16[1,2048,384]{2,1,0:T(8,128)(2,1)} %param.10), channel_id=1, source_target_pairs={{0,1},{1,0},{2,3},{3,2},{4,5},{5,4},{6,7},{7,6},{8,9},{9,8},{10,11... | collective-permute-start | bytes 4718600 | tf_op jit(solution)/shard_map/ppermute | solution.py:10
  90.5 99.4 %collective-permute-start.2 = (bf16[1,384,2048]{2,1,0:T(8,128)(2,1)S(1)}, bf16[1,384,2048]{2,1,0:T(8,128)(2,1)}, u32[]{:S(2)}, u32[]{:S(2)}) collective-permute-start(bf16[1,384,2048]{2,1,0:T(8,128)(2,1)S(1)} %copy-done.3), channel_id=1, source_target_pairs={{0,1},{1,0},{2,3},{3,2},{4,5},{5,4},{6,7},{7,6},{8,9},{9,8},{10,11... | collective-permute-start | bytes 4718600 | tf_op jit(solution)/shard_map/ppermute | solution.py:10
  90.9 98.9 %collective-permute-start = (bf16[1,2048,384]{2,1,0:T(8,128)(2,1)S(1)}, bf16[1,2048,384]{2,1,0:T(8,128)(2,1)}, u32[]{:S(2)}, u32[]{:S(2)}) collective-permute-start(bf16[1,2048,384]{2,1,0:T(8,128)(2,1)S(1)} %copy-done.2), channel_id=1, source_target_pairs={{0,1},{1,0},{2,3},{3,2},{4,5},{5,4},{6,7},{7,6},{8,9},{9,8},{10,11... | collective-permute-start | bytes 4718600 | tf_op jit(solution)/shard_map/ppermute | solution.py:10
  224.7 5.3 %copy-start.1 = (f32[256,8]{0,1:T(8,128)S(1)}, f32[256,8]{0,1:T(8,128)}, u32[]{:S(2)}) copy-start(f32[256,8]{0,1:T(8,128)} %param.8) | copy-start | bytes 24580
  224.7 5.3 %copy-start = (s32[256,8]{0,1:T(8,128)S(1)}, s32[256,8]{0,1:T(8,128)}, u32[]{:S(2)}) copy-start(s32[256,8]{0,1:T(8,128)} %param.7) | copy-start | bytes 24580
  224.7 97.7 %all-to-all-start.1 = ((bf16[4,1,256,2048]{3,2,1,0:T(8,128)(2,1)}), bf16[4,1,256,2048]{3,2,1,0:T(8,128)(2,1)}, u32[]{:S(2)}, u32[]{:S(2)}) async-start(bf16[4,1,256,2048]{3,2,1,0:T(8,128)(2,1)} %fusion.4), calls=%async_computation.1 | async-start | bytes 8388608 | tf_op jit(solution)/shard_map/all_to_all | solution.py:59
  229.7 162.6 %reduce-scatter.2.cloned.1.call-start = ((), (), s32[]{:S(2)}) async-start(), calls=%async_computation.4 | async-start | bytes 2621440 | tf_op jit(solution)/shard_map/reduce_scatter | solution.py:67
Sparse Core Ops, SparseCore 0:
  9.2 29.1 all-gather.1
  359.0 33.3 reduce-scatter.1
where the time goes:
time: 402 us; the launch traced here: 401 us
  waiting for transfers between devices  247 us (61%)
  local copies, waits for them, and re-layouts  71.9 us (18%)
  matrix products  32.7 us (8%)
  other arithmetic  24.3 us (6%)
  between operations  13.6 us (3%)
  starting transfers between devices  11.3 us (3%)
    all_to_all x1, waiting for transfers between devices, body(): lax.all_to_all(answer, 'expert', split_axis=0, concat_axis=0, tiled=True)  92.3 us
    all_to_all x1, waiting for transfers between devices, body(): lax.all_to_all(outgoing, 'expert', split_axis=0, concat_axis=0, tiled=True)  88.2 us
    scatter x1, local copies, waits for them, and re-layouts, body(): jnp.zeros((buckets * slots + 1, width), jnp.bfloat16).at[target]  41.8 us
    reduce_scatter x1, waiting for transfers between devices, body(): lax.psum_scatter(combined, 'tensor', scatter_dimension=1, tiled=True)  33.5 us
    all_gather x1, waiting for transfers between devices, body(): whole = lax.all_gather(tokens, 'tensor', axis=1, tiled=True)  28.1 us
    dot_general x2, matrix products, expert_partial(): jnp.einsum('...ecf,efd->...ecd', hidden, down_w, preferred_element_type=j...  20.9 us
    gather x1, local copies, waits for them, and re-layouts, body(): picked = flat_back[target].reshape(tok_rows, top, width)  19.1 us
    reduce_sum x1, other arithmetic, body(): jnp.sum(picked.astype(jnp.float32) * share_mine[:, :, None], axis=1)  12.6 us
  transfers between devices with their start and end apart: 7, of which 5 were waited for; matrix products, arithmetic and copies ran while one was open for 2% of the time, Pallas kernels for 0%

commit v1 on v0

--- a/solution.py
+++ b/solution.py
@@ -69,6 +69,36 @@
     )
 
 
+def dense_body(tokens, expert_ids, router_scores, w_gate, w_up, w_down):
+    tok_rows, top = expert_ids.shape
+    n_tensor = lax.axis_size("tensor")
+    shares = router_scores / jnp.sum(router_scores, axis=1, keepdims=True)
+    number = jnp.arange(lax.axis_size("expert") * n_tensor, dtype=jnp.int32)
+    table = jnp.sum(
+        jnp.where(expert_ids[:, :, None] == number, shares[:, :, None], 0.0), axis=1
+    )
+    tables = lax.all_gather(table, "expert", axis=0, tiled=True)
+    expert = lax.axis_index("expert") * n_tensor + lax.axis_index("tensor")
+    weight = jnp.sum(jnp.where(number == expert, tables, 0.0), axis=1)
+    other_gate, other_up, other_down = from_partner((w_gate, w_up, w_down), "seq", 0)
+    rows = lax.all_gather(tokens, "expert", axis=0, tiled=True)
+    whole = lax.all_gather(rows, "tensor", axis=1, tiled=True)[None]
+    own_part = expert_partial(whole, w_gate, w_up, w_down)
+    far_part = expert_partial(whole, other_gate, other_up, other_down)
+    answer = ((own_part + far_part)[0] * weight[:, None]).astype(jnp.bfloat16)
+    part = lax.psum_scatter(answer, "tensor", scatter_dimension=1, tiled=True)
+    return lax.psum_scatter(part, "expert", scatter_dimension=0, tiled=True)
+
+
+def pick_body(tokens, expert_ids, router_scores, w_gate, w_up, w_down):
+    tok_rows, top = expert_ids.shape
+    exp_dev = w_gate.shape[0]
+    experts_all = exp_dev * lax.axis_size("expert") * lax.axis_size("tensor")
+    slots = min(tok_rows, max(2, tok_rows * top * 2 // experts_all))
+    plan = dense_body if exp_dev == 1 and slots == tok_rows else body
+    return plan(tokens, expert_ids, router_scores, w_gate, w_up, w_down)
+
+
 def solution(mesh):
     placed = (
         P(("groups", "expert", "seq"), "tensor"),
@@ -79,7 +109,7 @@
         P(("expert", "tensor"), "seq", None),
     )
     return jax.shard_map(
-        body,
+        pick_body,
         mesh=mesh,
         in_specs=placed,
         out_specs=P(("groups", "expert", "seq"), "tensor"),

time: 402 us -> 215 us (0.53)
  waiting for transfers between devices: 247 us -> 153 us
  local copies, waits for them, and re-layouts: 71.9 us -> 0.01 us
  other arithmetic: 24.3 us -> 2.23 us
  blocking collectives: 0 us -> 13.1 us
  starting transfers between devices: 11.3 us -> 0.77 us
    all_to_all x2 -> x0, waiting for transfers between devices: 180 us -> none  [the longest x1 92.3 us: body(): lax.all_to_all(answer, 'expert', split_axis=0, concat_axis=0, tiled=True)]
    reduce_scatter x1 -> x2, waiting for transfers between devices: 33.5 us -> 82.2 us  [the longest x1 52.8 us: dense_body(): part = lax.psum_scatter(answer, 'tensor', scatter_dimension=1, tiled=True)]
    all_gather x1 -> x2, waiting for transfers between devices: 28.1 us -> 70.1 us  [the longest x1 37.8 us: dense_body(): whole = lax.all_gather(rows, 'tensor', axis=1, tiled=True)[None]]
    scatter x1 -> x0, local copies, waits for them, and re-layouts: 41.8 us -> none  [body(): jnp.zeros((buckets * slots + 1, width), jnp.bfloat16).at[target]]
    gather x1 -> x0, local copies, waits for them, and re-layouts: 19.1 us -> none  [body(): picked = flat_back[target].reshape(tok_rows, top, width)]
    all_gather x0 -> x1, blocking collectives: none -> 13.1 us  [dense_body(): tables = lax.all_gather(table, 'expert', axis=0, tiled=True)]
    reduce_sum x3, other arithmetic: 12.6 us -> 1.52 us  [the longest x1 0.72 us: dense_body(): jnp.sum(jnp.where(expert_ids[:, :, None] == number, shares[:, :, None], 0...]
    all_to_all x2 -> x0, starting transfers between devices: 10.4 us -> none  [the longest x1 5.38 us: body(): lax.all_to_all(outgoing, 'expert', split_axis=0, concat_axis=0, tiled=True)]
  transfers between devices with their start and end apart: 7 -> 7, of which waited for: 5 -> 4; matrix products, arithmetic and copies ran while one was open for 2% -> 11% of each run, Pallas kernels for 0% -> 0%
where the time goes in v1:
time: 215 us
  waiting for transfers between devices  153 us (71%)
  matrix products  32.7 us (15%)
  between operations  13.2 us (6%)
  blocking collectives  13.1 us (6%)
  other arithmetic  2.23 us (1%)
    reduce_scatter x1, waiting for transfers between devices, dense_body(): part = lax.psum_scatter(answer, 'tensor', scatter_dimension=1, tiled=True)  52.8 us
    all_gather x1, waiting for transfers between devices, dense_body(): whole = lax.all_gather(rows, 'tensor', axis=1, tiled=True)[None]  37.8 us
    all_gather x1, waiting for transfers between devices, dense_body(): rows = lax.all_gather(tokens, 'expert', axis=0, tiled=True)  32.3 us
    reduce_scatter x1, waiting for transfers between devices, dense_body(): return lax.psum_scatter(part, 'expert', scatter_dimension=0, tiled=True)  29.4 us
    dot_general x2, matrix products, expert_partial(): jnp.einsum('...ecf,efd->...ecd', hidden, down_w, preferred_element_type=j...  21.4 us
    all_gather x1, blocking collectives, dense_body(): tables = lax.all_gather(table, 'expert', axis=0, tiled=True)  13.1 us
    dot_general x1, matrix products, expert_partial(): jnp.einsum('...ecd,edf->...ecf', block, gate_w, preferred_element_type=jn...  6.29 us
    dot_general x1, matrix products, expert_partial(): jnp.einsum('...ecd,edf->...ecf', block, up_w, preferred_element_type=jnp....  5.04 us
  transfers between devices with their start and end apart: 7, of which 4 were waited for; matrix products, arithmetic and copies ran while one was open for 11% of the time, Pallas kernels for 0%

profile of v1, /device:TPU:0, one launch (start us, length us, event | category | flops | bytes accessed | tf_op | source)
XLA Modules:
  0.0 215.0 jit_solution(14086361324068002685)
XLA Ops:
  6.5 0.7 all-gather.3.cloned.1.call-update
  7.3 0.0 all-gather.5.cloned.1.call-start
  7.3 32.3 %all-gather.3.cloned.1.call-done = bf16[1024,512]{1,0:T(8,128)(2,1)} async-done(((bf16[256,512]{1,0:T(8,128)(2,1)}), bf16[1024,512]{1,0:T(8,128)(2,1)}) %all-gather.3.cloned.1.call-update) | async-done | bytes 1048592 | tf_op jit(solution)/shard_map/all_gather | solution.py:84
  39.6 0.0 all-gather.5.cloned.1.call-update
  39.6 0.0 reduce-scatter.3.cloned.1.call-start
  39.7 0.1 collective-permute-start.1
  39.7 0.5 collective-permute-start
  40.2 0.1 collective-permute-start.2
  40.3 0.7 reduce_sum.27
  41.0 0.7 broadcast_divide_fusion
  41.7 0.7 select_reduce_fusion
  42.5 13.1 %all_gather.11 = f32[1024,16]{0,1:T(8,128)S(1)} all-gather(f32[256,16]{0,1:T(8,128)S(1)} %select_reduce_fusion), channel_id=1, replica_groups=mesh['groups'=1,'expert'=4,'tensor'=4,'seq'=2] {'expert'}, dimensions={0}, use_global_device_ids=true | all-gather | bytes 81920 | tf_op jit(solution)/shard_map/all_gather | solution.py:80
  55.6 0.1 select_reduce_fusion.1
  55.7 37.8 %all-gather.5.cloned.1.call-done = bf16[1024,2048]{1,0:T(8,128)(2,1)} async-done(((bf16[1024,512]{1,0:T(8,128)(2,1)}), bf16[1024,2048]{1,0:T(8,128)(2,1)}) %all-gather.5.cloned.1.call-update) | async-done | bytes 4194320 | tf_op jit(solution)/shard_map/all_gather | solution.py:85
  93.5 6.3 %fusion.9 = f32[1024,384]{1,0:T(8,128)} fusion(bf16[1024,2048]{1,0:T(8,128)(2,1)} %all-gather.5.cloned.1.call-done, bf16[1,2048,384]{2,1,0:T(8,128)(2,1)} %param.9), kind=kOutput, calls=%fused_computation.10 | convolution fusion | flops 1610612736 | bytes 7340032 | tf_op jit(solution)/shard_map/...ecd,edf->...ecf/dot_general | solution.py:14
  99.8 5.0 %fusion.1 = f32[1024,384]{1,0:T(8,128)} fusion(bf16[1024,2048]{1,0:T(8,128)(2,1)S(1)} %copy-done, bf16[1,2048,384]{2,1,0:T(8,128)(2,1)} %collective-permute-done.1), kind=kOutput, calls=%fused_computation.2 | convolution fusion | flops 1610612736 | bytes 7340032 | tf_op jit(solution)/shard_map/...ecd,edf->...ecf/dot_general | solution.py:15
  104.9 10.4 %fusion.5 = f32[1024,2048]{1,0:T(8,128)} fusion(bf16[1,384,2048]{2,1,0:T(8,128)(2,1)S(1)} %copy-done.2, f32[1024,384]{1,0:T(8,128)} %fusion.9, bf16[1024,2048]{1,0:T(8,128)(2,1)} %all-gather.5.cloned.1.call-done, bf16[1,2048,384]{2,1,0:T(8,128)(2,1)S(1)} %copy-done.1), kind=kOutput, calls=%fused_computation.6 | convolution fusion | flops 3223584768 | bytes 17301504 | tf_op jit(solution)/shard_map/...ecf,efd->...ecd/dot_general | solution.py:17
  115.3 0.0 collective-permute-done
  115.3 10.9 %multiply_convert_fusion = bf16[1024,2048]{1,0:T(8,128)(2,1)} fusion(f32[1024,2048]{1,0:T(8,128)} %fusion.5, f32[1024]{0:T(1024)S(1)} %select_reduce_fusion.1, bf16[1,384,2048]{2,1,0:T(8,128)(2,1)} %collective-permute-done.2, f32[1024,384]{1,0:T(8,128)} %fusion.1, bf16[1024,2048]{1,0:T(8,128)(2,1)} %all-gather.5.cloned.1.call-done, ...), kind=kOutput, calls=%fused_computation | convolution fusion | flops 3229876224 | bytes 21499904 | tf_op jit(solution)/shard_map/...ecf,efd->...ecd/dot_general | solution.py:17
  126.2 0.0 reduce-scatter.3.cloned.1.call-update
  126.3 0.0 reduce-scatter.5.cloned.1.call-start
  126.3 52.8 %reduce-scatter.3.cloned.1.call-done = bf16[1024,512]{1,0:T(8,128)(2,1)} async-done(((bf16[1024,2048]{1,0:T(8,128)(2,1)}), bf16[1024,512]{1,0:T(8,128)(2,1)}) %reduce-scatter.3.cloned.1.call-update) | async-done | bytes 1048592 | tf_op jit(solution)/shard_map/reduce_scatter | solution.py:89
  179.1 0.0 reduce-scatter.5.cloned.1.call-update
  179.1 29.4 %reduce-scatter.5.cloned.1.call-done = bf16[256,512]{1,0:T(8,128)(2,1)} async-done(((bf16[1024,512]{1,0:T(8,128)(2,1)}), bf16[256,512]{1,0:T(8,128)(2,1)}) %reduce-scatter.5.cloned.1.call-update) | async-done | bytes 262160 | tf_op jit(solution)/shard_map/reduce_scatter | solution.py:90
  (10 shorter events, 0.0 us)
Async XLA Ops:
  6.5 33.1 %all-gather.3.cloned.1.call-start = ((), (), s32[]{:S(2)}) async-start(), calls=%async_computation.2 | async-start | bytes 1310720 | tf_op jit(solution)/shard_map/all_gather | solution.py:84
  7.3 86.2 %all-gather.5.cloned.1.call-start = ((), (), s32[]{:S(2)}) async-start(), calls=%async_computation.3 | async-start | bytes 5242880 | tf_op jit(solution)/shard_map/all_gather | solution.py:85
  39.6 139.5 %reduce-scatter.3.cloned.1.call-start = ((), (), s32[]{:S(2)}) async-start(), calls=%async_computation.4 | async-start | bytes 5242880 | tf_op jit(solution)/shard_map/reduce_scatter | solution.py:89
  39.7 60.1 %collective-permute-start.1 = (bf16[1,2048,384]{2,1,0:T(8,128)(2,1)}, bf16[1,2048,384]{2,1,0:T(8,128)(2,1)}, u32[]{:S(2)}, u32[]{:S(2)}) collective-permute-start(bf16[1,2048,384]{2,1,0:T(8,128)(2,1)} %param.10), channel_id=1, source_target_pairs={{0,1},{1,0},{2,3},{3,2},{4,5},{5,4},{6,7},{7,6},{8,9},{9,8},{10,11... | collective-permute-start | bytes 4718600 | tf_op jit(solution)/shard_map/ppermute | solution.py:10
  39.7 75.6 %collective-permute-start = (bf16[1,2048,384]{2,1,0:T(8,128)(2,1)}, bf16[1,2048,384]{2,1,0:T(8,128)(2,1)}, u32[]{:S(2)}, u32[]{:S(2)}) collective-permute-start(bf16[1,2048,384]{2,1,0:T(8,128)(2,1)} %param.9), channel_id=1, source_target_pairs={{0,1},{1,0},{2,3},{3,2},{4,5},{5,4},{6,7},{7,6},{8,9},{9,8},{10,11... | collective-permute-start | bytes 4718600 | tf_op jit(solution)/shard_map/ppermute | solution.py:10
  40.2 75.1 %collective-permute-start.2 = (bf16[1,384,2048]{2,1,0:T(8,128)(2,1)}, bf16[1,384,2048]{2,1,0:T(8,128)(2,1)}, u32[]{:S(2)}, u32[]{:S(2)}) collective-permute-start(bf16[1,384,2048]{2,1,0:T(8,128)(2,1)} %param.11), channel_id=1, source_target_pairs={{0,1},{1,0},{2,3},{3,2},{4,5},{5,4},{6,7},{7,6},{8,9},{9,8},{10,11... | collective-permute-start | bytes 4718600 | tf_op jit(solution)/shard_map/ppermute | solution.py:10
  93.5 6.3 %copy-start = (bf16[1024,2048]{1,0:T(8,128)(2,1)S(1)}, bf16[1024,2048]{1,0:T(8,128)(2,1)}, u32[]{:S(2)}) copy-start(bf16[1024,2048]{1,0:T(8,128)(2,1)} %all-gather.5.cloned.1.call-done) | copy-start | bytes 12582916
  99.8 5.1 %copy-start.1 = (bf16[1,2048,384]{2,1,0:T(8,128)(2,1)S(1)}, bf16[1,2048,384]{2,1,0:T(8,128)(2,1)}, u32[]{:S(2)}) copy-start(bf16[1,2048,384]{2,1,0:T(8,128)(2,1)} %param.10) | copy-start | bytes 4718596
  99.8 5.1 %copy-start.2 = (bf16[1,384,2048]{2,1,0:T(8,128)(2,1)S(1)}, bf16[1,384,2048]{2,1,0:T(8,128)(2,1)}, u32[]{:S(2)}) copy-start(bf16[1,384,2048]{2,1,0:T(8,128)(2,1)} %param.11) | copy-start | bytes 4718596
  126.3 82.2 %reduce-scatter.5.cloned.1.call-start = ((), (), s32[]{:S(2)}) async-start(), calls=%async_computation.5 | async-start | bytes 1310720 | tf_op jit(solution)/shard_map/reduce_scatter | solution.py:90
Sparse Core Ops, SparseCore 0:
  8.9 30.6 all-gather.2
  41.4 52.0 all-gather.4
  126.4 52.6 reduce-scatter.2
  181.3 27.0 reduce-scatter.4

commit v2 on v0

--- a/solution.py
+++ b/solution.py
@@ -1,6 +1,8 @@
 import jax
 import jax.numpy as jnp
 from jax import lax
+from jax.experimental import pallas as pl
+from jax.experimental.pallas import tpu as pltpu
 from jax.sharding import PartitionSpec as P
 
 
@@ -69,6 +71,224 @@
     )
 
 
+def dense_kernel(
+    tokens, table, gate_w, up_w, down_w, out,
+    rows, tables, gate_all, up_all, down_all, hidden, part,
+    diag, joined, side, final, back, send, recv, local,
+):
+    n_rows, cols = tokens.shape
+    half = n_rows // 2
+    units = gate_w.shape[2]
+    z = lax.axis_index("expert")
+    t = lax.axis_index("tensor")
+    s = lax.axis_index("seq")
+    tx, ty, td = t + 1 - 2 * (t % 2), (t + 2) % 4, 3 - t
+    beside = ({"tensor": tx}, {"tensor": ty})
+    along = (None, {"expert": z + 1 - 2 * (z % 2)}, {"expert": (z + 2) % 4}, {"expert": 3 - z})
+    partner = {"seq": 1 - s}
+    low, high, full = pl.ds(0, half), pl.ds(half, half), pl.ds(0, n_rows)
+
+    def span(index):
+        return pl.ds(pl.multiple_of(index * cols, cols), cols)
+
+    barrier = pltpu.get_barrier_semaphore()
+    for device in (partner,) + beside + along[1:]:
+        pl.semaphore_signal(barrier, inc=1, device_id=device, device_id_type=pl.DeviceIdType.MESH)
+    pl.semaphore_wait(barrier, 6)
+
+    def remote(source, target, number, device):
+        return pltpu.make_async_remote_copy(
+            src_ref=source,
+            dst_ref=target,
+            send_sem=send.at[number],
+            recv_sem=recv.at[number],
+            device_id=device,
+            device_id_type=pl.DeviceIdType.MESH,
+        )
+
+    mine = span(t)
+    to_z = [None] + [remote(tokens, rows.at[j, :, mine], 2 + j, along[j]) for j in (1, 2, 3)]
+    table_z = [None] + [remote(table, tables.at[j], 5 + j, along[j]) for j in (1, 2, 3)]
+    direct, passed, ahead, plain, summed = [], [], [], [], []
+    for j in range(4):
+        block = rows.at[j, :, mine]
+        origin = tokens if j == 0 else block
+        direct.append([remote(origin, block, 9 + 2 * j + d, beside[d]) for d in (0, 1)])
+        passed.append([
+            remote(rows.at[j, high, span(ty)], rows.at[j, high, span(ty)], 17 + 2 * j, beside[0]),
+            remote(rows.at[j, low, span(tx)], rows.at[j, low, span(tx)], 18 + 2 * j, beside[1]),
+        ])
+        ahead.append([
+            remote(part.at[j, low, span(td)], diag.at[j, 0], 25 + 2 * j, beside[0]),
+            remote(part.at[j, high, span(td)], diag.at[j, 1], 26 + 2 * j, beside[1]),
+        ])
+        plain.append([
+            remote(part.at[j, low, span(tx)], side.at[j, 0, low], 33 + 2 * j, beside[0]),
+            remote(part.at[j, high, span(ty)], side.at[j, 1, high], 34 + 2 * j, beside[1]),
+        ])
+        summed.append([
+            remote(joined.at[j, 0], side.at[j, 0, high], 41 + 2 * j, beside[0]),
+            remote(joined.at[j, 1], side.at[j, 1, low], 42 + 2 * j, beside[1]),
+        ])
+    to_home = [None] + [remote(final.at[j], back.at[j], 48 + j, along[j]) for j in (1, 2, 3)]
+    weights = [
+        remote(gate_w.at[0], gate_all.at[:, pl.ds(units, units)], 0, partner),
+        remote(up_w.at[0], up_all.at[:, pl.ds(units, units)], 1, partner),
+        remote(down_w.at[0], down_all.at[pl.ds(units, units)], 2, partner),
+    ]
+    loads = [
+        pltpu.make_async_copy(tokens, rows.at[0, :, mine], local.at[0]),
+        pltpu.make_async_copy(gate_w.at[0], gate_all.at[:, pl.ds(0, units)], local.at[1]),
+        pltpu.make_async_copy(up_w.at[0], up_all.at[:, pl.ds(0, units)], local.at[2]),
+        pltpu.make_async_copy(down_w.at[0], down_all.at[pl.ds(0, units)], local.at[3]),
+        pltpu.make_async_copy(table, tables.at[0], local.at[4]),
+    ]
+
+    def start(copies):
+        for copy in copies:
+            copy.start()
+
+    def arrive(copies):
+        for copy in copies:
+            copy.wait_recv()
+
+    def spread(j):
+        to_z[j].wait_recv()
+        start(direct[j])
+
+    def pass_on(j):
+        arrive(direct[j])
+        start(passed[j])
+
+    def answer(j, sending):
+        arrive(passed[j])
+
+        def inner(c, carry):
+            at = pl.ds(pl.multiple_of(c * 256, 256), 256)
+            gate = jnp.dot(rows[j], gate_all[:, at], preferred_element_type=jnp.float32)
+            upper = jnp.dot(rows[j], up_all[:, at], preferred_element_type=jnp.float32)
+            hidden[:, at] = (gate * jax.nn.sigmoid(gate) * upper).astype(jnp.bfloat16)
+            return carry
+
+        lax.fori_loop(0, 2 * units // 256, inner, 0)
+        share = tables[j, pl.ds(z * 4 + t, 1), :]
+        share = jnp.broadcast_to(share, (128, n_rows)).T[:, :1]
+        for index, copies in ((td, ahead[j]), (tx, plain[j][:1]), (ty, plain[j][1:]), (t, [])):
+            value = jnp.dot(hidden[...], down_all[:, span(index)], preferred_element_type=jnp.float32)
+            part[j, :, span(index)] = (value * share).astype(jnp.bfloat16)
+            if sending:
+                start(copies)
+
+    def join(j):
+        arrive(ahead[j])
+        upper_rows = part[j, high, span(tx)].astype(jnp.float32) + diag[j, 1].astype(jnp.float32)
+        joined[j, 0] = upper_rows.astype(jnp.bfloat16)
+        lower_rows = part[j, low, span(ty)].astype(jnp.float32) + diag[j, 0].astype(jnp.float32)
+        joined[j, 1] = lower_rows.astype(jnp.bfloat16)
+        start(summed[j])
+
+    def gathered(j):
+        arrive(plain[j] + summed[j])
+        return (
+            part[j, :, mine].astype(jnp.float32)
+            + side[j, 0].astype(jnp.float32)
+            + side[j, 1].astype(jnp.float32)
+        )
+
+    def go_home(j):
+        final[j] = gathered(j).astype(jnp.bfloat16)
+        to_home[j].start()
+
+    start(direct[0])
+    start(to_z[1:])
+    start(table_z[1:])
+    start(weights)
+    start(loads)
+    spread(1)
+    pass_on(0)
+    spread(2)
+    for copy in loads:
+        copy.wait()
+    arrive(weights + table_z[1:])
+    answer(0, False)
+    pass_on(1)
+    spread(3)
+    answer(1, True)
+    pass_on(2)
+    answer(2, True)
+    join(1)
+    pass_on(3)
+    start(ahead[0] + plain[0])
+    answer(3, True)
+    join(2)
+    go_home(1)
+    join(3)
+    go_home(2)
+    join(0)
+    go_home(3)
+    total = gathered(0)
+    arrive(to_home[1:])
+    for j in (1, 2, 3):
+        total = total + back[j].astype(jnp.float32)
+    out[...] = total.astype(jnp.bfloat16)
+    everything = to_z[1:] + table_z[1:] + weights + to_home[1:]
+    for group in direct + passed + ahead + plain + summed:
+        everything = everything + group
+    for copy in everything:
+        copy.wait_send()
+
+
+def dense_body(tokens, expert_ids, router_scores, w_gate, w_up, w_down):
+    n_rows, cols = tokens.shape
+    _, width, units = w_gate.shape
+    half = n_rows // 2
+    shares = router_scores / jnp.sum(router_scores, axis=1, keepdims=True)
+    number = jnp.arange(16, dtype=jnp.int32)[:, None, None]
+    table = jnp.sum(jnp.where(expert_ids.T[None] == number, shares.T[None], 0.0), axis=1)
+    bf16 = jnp.bfloat16
+    return pl.pallas_call(
+        dense_kernel,
+        out_shape=jax.ShapeDtypeStruct((n_rows, cols), bf16),
+        in_specs=[pl.BlockSpec(memory_space=pl.ANY)] * 5,
+        out_specs=pl.BlockSpec(memory_space=pltpu.VMEM),
+        scratch_shapes=[
+            pltpu.VMEM((4, n_rows, width), bf16),
+            pltpu.VMEM((4, 16, n_rows), jnp.float32),
+            pltpu.VMEM((width, 2 * units), bf16),
+            pltpu.VMEM((width, 2 * units), bf16),
+            pltpu.VMEM((2 * units, width), bf16),
+            pltpu.VMEM((n_rows, 2 * units), bf16),
+            pltpu.VMEM((4, n_rows, width), bf16),
+            pltpu.VMEM((4, 2, half, cols), bf16),
+            pltpu.VMEM((4, 2, half, cols), bf16),
+            pltpu.VMEM((4, 2, n_rows, cols), bf16),
+            pltpu.VMEM((4, n_rows, cols), bf16),
+            pltpu.VMEM((4, n_rows, cols), bf16),
+            pltpu.SemaphoreType.DMA((52,)),
+            pltpu.SemaphoreType.DMA((52,)),
+            pltpu.SemaphoreType.DMA((5,)),
+        ],
+        compiler_params=pltpu.CompilerParams(
+            collective_id=0, has_side_effects=True, vmem_limit_bytes=44 * 1024 * 1024
+        ),
+        cost_estimate=pl.CostEstimate(
+            flops=4 * n_rows * 6 * width * 2 * units,
+            bytes_accessed=6 * width * units * 2,
+            transcendentals=4 * n_rows * 2 * units,
+        ),
+    )(tokens, table, w_gate, w_up, w_down)
+
+
+def pick_body(tokens, expert_ids, router_scores, w_gate, w_up, w_down):
+    tok_rows, top = expert_ids.shape
+    exp_dev = w_gate.shape[0]
+    n_owner, n_tensor = lax.axis_size("expert"), lax.axis_size("tensor")
+    slots = min(tok_rows, max(2, tok_rows * top * 2 // (exp_dev * n_owner * n_tensor)))
+    dense = exp_dev == 1 and n_owner == 4 and n_tensor == 4 and slots == tok_rows
+    plan = dense_body if dense else body
+    return plan(tokens, expert_ids, router_scores, w_gate, w_up, w_down)
+
+
 def solution(mesh):
     placed = (
         P(("groups", "expert", "seq"), "tensor"),
@@ -79,7 +299,7 @@
         P(("expert", "tensor"), "seq", None),
     )
     return jax.shard_map(
-        body,
+        pick_body,
         mesh=mesh,
         in_specs=placed,
         out_specs=P(("groups", "expert", "seq"), "tensor"),

time: 402 us -> 109 us (0.27)
  the two profiles are of different devices: /device:TPU:0 before, /device:TPU:8 now
where the time goes in v2:
time: 109 us
  Pallas kernels  101 us (93%)
  local copies, waits for them, and re-layouts  5.87 us (5%)
  other arithmetic  2.15 us (2%)
    pallas_call x1, Pallas kernels, dense_body(): pl.pallas_call(dense_kernel, out_shape=jax.ShapeDtypeStruct((n_rows, cols...  101 us
    unnamed x9, local copies, waits for them, and re-layouts  5.87 us

profile of v2, /device:TPU:8, one launch (start us, length us, event | category | flops | bytes accessed | tf_op | source)
XLA Modules:
  0.0 108.6 jit_solution(12795536593807171492)
XLA Ops:
  0.0 0.7 reduce_sum.18
  0.7 0.7 divide_bitcast_fusion
  1.4 0.7 select_reduce_fusion.table
  2.2 0.0 copy-start
  2.2 1.4 %copy-done = bf16[1,2048,384]{2,1,0:T(8,128)(2,1)S(1)} copy-done((bf16[1,2048,384]{2,1,0:T(8,128)(2,1)S(1)}, bf16[1,2048,384]{2,1,0:T(8,128)(2,1)}, u32[]{:S(2)}) %copy-start) | copy-done | bytes 1572888
  3.6 0.0 copy-start.1
  3.6 1.4 %copy-done.1 = bf16[1,2048,384]{2,1,0:T(8,128)(2,1)S(1)} copy-done((bf16[1,2048,384]{2,1,0:T(8,128)(2,1)S(1)}, bf16[1,2048,384]{2,1,0:T(8,128)(2,1)}, u32[]{:S(2)}) %copy-start.1) | copy-done | bytes 1572888
  5.0 0.0 copy-start.2
  5.0 1.4 %copy-done.2 = bf16[1,384,2048]{2,1,0:T(8,128)(2,1)S(1)} copy-done((bf16[1,384,2048]{2,1,0:T(8,128)(2,1)S(1)}, bf16[1,384,2048]{2,1,0:T(8,128)(2,1)}, u32[]{:S(2)}) %copy-start.2) | copy-done | bytes 1572888
  6.4 0.0 copy-start.3
  6.4 0.9 copy-done.3
  7.3 100.6 %shard_map.64 = bf16[256,512]{1,0:T(8,128)(2,1)S(1)} custom-call(bf16[256,512]{1,0:T(8,128)(2,1)S(1)} %copy-done.3, f32[16,256]{1,0:T(8,128)S(1)} %select_reduce_fusion.table, bf16[1,2048,384]{2,1,0:T(8,128)(2,1)S(1)} %copy-done, bf16[1,2048,384]{2,1,0:T(8,128)(2,1)S(1)} %copy-done.1, bf16[1,384,2048]{2,1,0:T(8,128)(2,1)S(1)} %copy-done.2), custom_call_target="tpu_custom_call" | custom-call | flops 9663676416 | bytes 9437184 | tf_op jit(solution)/shard_map/pallas_call | solution.py:249
  107.9 0.7 copy.8
Async XLA Ops:
  2.2 1.4 %copy-start = (bf16[1,2048,384]{2,1,0:T(8,128)(2,1)S(1)}, bf16[1,2048,384]{2,1,0:T(8,128)(2,1)}, u32[]{:S(2)}) copy-start(bf16[1,2048,384]{2,1,0:T(8,128)(2,1)} %gate_w.1) | copy-start | bytes 4718596
  3.6 1.4 %copy-start.1 = (bf16[1,2048,384]{2,1,0:T(8,128)(2,1)S(1)}, bf16[1,2048,384]{2,1,0:T(8,128)(2,1)}, u32[]{:S(2)}) copy-start(bf16[1,2048,384]{2,1,0:T(8,128)(2,1)} %up_w.1) | copy-start | bytes 4718596
  5.0 1.4 %copy-start.2 = (bf16[1,384,2048]{2,1,0:T(8,128)(2,1)S(1)}, bf16[1,384,2048]{2,1,0:T(8,128)(2,1)}, u32[]{:S(2)}) copy-start(bf16[1,384,2048]{2,1,0:T(8,128)(2,1)} %down_w.1) | copy-start | bytes 4718596
  6.4 0.9 copy-start.3

commit v3 on v2

--- a/solution.py
+++ b/solution.py
@@ -130,6 +130,10 @@
             remote(joined.at[j, 0], side.at[j, 0, high], 41 + 2 * j, beside[0]),
             remote(joined.at[j, 1], side.at[j, 1, low], 42 + 2 * j, beside[1]),
         ])
+    relay = [
+        remote(rows.at[0, :, span(index)], rows.at[1, :, span(index)], 52 + i, along[1])
+        for i, index in enumerate((tx, ty, td))
+    ]
     to_home = [None] + [remote(final.at[j], back.at[j], 48 + j, along[j]) for j in (1, 2, 3)]
     weights = [
         remote(gate_w.at[0], gate_all.at[:, pl.ds(units, units)], 0, partner),
@@ -159,9 +163,13 @@
     def pass_on(j):
         arrive(direct[j])
         start(passed[j])
+        if j == 0:
+            start(relay[:2])
 
     def answer(j, sending):
-        arrive(passed[j])
+        arrive(to_z[1:2] + relay if j == 1 else passed[j])
+        if j == 0:
+            start(relay[2:])
 
         def inner(c, carry):
             at = pl.ds(pl.multiple_of(c * 256, 256), 256)
@@ -200,39 +208,37 @@
         to_home[j].start()
 
     start(direct[0])
-    start(to_z[1:])
+    start(to_z[2:] + to_z[1:2])
     start(table_z[1:])
     start(weights)
     start(loads)
-    spread(1)
     pass_on(0)
     spread(2)
     for copy in loads:
         copy.wait()
     arrive(weights + table_z[1:])
     answer(0, False)
-    pass_on(1)
+    pass_on(2)
     spread(3)
-    answer(1, True)
-    pass_on(2)
     answer(2, True)
-    join(1)
     pass_on(3)
-    start(ahead[0] + plain[0])
     answer(3, True)
     join(2)
-    go_home(1)
+    start(ahead[0] + plain[0])
+    answer(1, True)
     join(3)
     go_home(2)
+    join(1)
+    go_home(3)
     join(0)
-    go_home(3)
+    go_home(1)
     total = gathered(0)
     arrive(to_home[1:])
     for j in (1, 2, 3):
         total = total + back[j].astype(jnp.float32)
     out[...] = total.astype(jnp.bfloat16)
-    everything = to_z[1:] + table_z[1:] + weights + to_home[1:]
-    for group in direct + passed + ahead + plain + summed:
+    everything = to_z[1:] + relay + table_z[1:] + weights + to_home[1:]
+    for group in direct[:1] + direct[2:] + passed[:1] + passed[2:] + ahead + plain + summed:
         everything = everything + group
     for copy in everything:
         copy.wait_send()
@@ -249,7 +255,7 @@
     return pl.pallas_call(
         dense_kernel,
         out_shape=jax.ShapeDtypeStruct((n_rows, cols), bf16),
-        in_specs=[pl.BlockSpec(memory_space=pl.ANY)] * 5,
+        in_specs=[pl.BlockSpec(memory_space=pltpu.HBM)] * 5,
         out_specs=pl.BlockSpec(memory_space=pltpu.VMEM),
         scratch_shapes=[
             pltpu.VMEM((4, n_rows, width), bf16),
@@ -264,12 +270,12 @@
             pltpu.VMEM((4, 2, n_rows, cols), bf16),
             pltpu.VMEM((4, n_rows, cols), bf16),
             pltpu.VMEM((4, n_rows, cols), bf16),
-            pltpu.SemaphoreType.DMA((52,)),
-            pltpu.SemaphoreType.DMA((52,)),
+            pltpu.SemaphoreType.DMA((55,)),
+            pltpu.SemaphoreType.DMA((55,)),
             pltpu.SemaphoreType.DMA((5,)),
         ],
         compiler_params=pltpu.CompilerParams(
-            collective_id=0, has_side_effects=True, vmem_limit_bytes=44 * 1024 * 1024
+            collective_id=0, has_side_effects=True, vmem_limit_bytes=62 * 1024 * 1024
         ),
         cost_estimate=pl.CostEstimate(
             flops=4 * n_rows * 6 * width * 2 * units,

time: 109 us -> 96.4 us (0.88)
  the two profiles are of different devices: /device:TPU:8 before, /device:TPU:0 now
where the time goes in v3:
time: 96.4 us; the launch traced here: 96.1 us
  Pallas kernels  91.7 us (95%)
  other arithmetic  2.76 us (3%)
  local copies, waits for them, and re-layouts  1.67 us (2%)
    pallas_call x1, Pallas kernels, dense_body(): pl.pallas_call(dense_kernel, out_shape=jax.ShapeDtypeStruct((n_rows, cols...  91.7 us

profile of v3, /device:TPU:0, one launch (start us, length us, event | category | flops | bytes accessed | tf_op | source)
XLA Modules:
  0.0 96.1 jit_solution(7076372917795226222)
XLA Ops:
  0.0 0.7 reduce_sum.18
  0.7 0.7 divide_bitcast_fusion
  1.4 1.3 %select_reduce_fusion.table = f32[16,256]{1,0:T(8,128)} fusion(f32[8,256]{1,0:T(8,128)S(1)} %divide_bitcast_fusion, s32[8,256]{1,0:T(8,128)} %bitcast.3), kind=kLoop, calls=%fused_computation | loop fusion | flops 94208 | bytes 32768 | tf_op jit(solution)/shard_map/reduce_sum | solution.py:253
  2.8 91.7 %shard_map.64 = bf16[256,512]{1,0:T(8,128)(2,1)} custom-call(bf16[256,512]{1,0:T(8,128)(2,1)} %tokens.1, f32[16,256]{1,0:T(8,128)} %select_reduce_fusion.table, bf16[1,2048,384]{2,1,0:T(8,128)(2,1)} %gate_w.1, bf16[1,2048,384]{2,1,0:T(8,128)(2,1)} %up_w.1, bf16[1,384,2048]{2,1,0:T(8,128)(2,1)} %down_w.1), custom_call_target="tpu_custom_call" | custom-call | flops 9663676416 | bytes 9437184 | tf_op jit(solution)/shard_map/pallas_call | solution.py:255
  94.4 1.7 %copy.8 = bf16[256,512]{1,0:T(8,128)(2,1)} copy(bf16[256,512]{1,0:T(8,128)(2,1)} %shard_map.64) | data formatting | bytes 524288

commit v4 on v3

--- a/solution.py
+++ b/solution.py
@@ -72,7 +72,7 @@
 
 
 def dense_kernel(
-    tokens, table, gate_w, up_w, down_w, out,
+    tokens, ids, scores, gate_w, up_w, down_w, out,
     rows, tables, gate_all, up_all, down_all, hidden, part,
     diag, joined, side, final, back, send, recv, local,
 ):
@@ -108,7 +108,7 @@
 
     mine = span(t)
     to_z = [None] + [remote(tokens, rows.at[j, :, mine], 2 + j, along[j]) for j in (1, 2, 3)]
-    table_z = [None] + [remote(table, tables.at[j], 5 + j, along[j]) for j in (1, 2, 3)]
+    table_z = [None] + [remote(tables.at[0], tables.at[j], 5 + j, along[j]) for j in (1, 2, 3)]
     direct, passed, ahead, plain, summed = [], [], [], [], []
     for j in range(4):
         block = rows.at[j, :, mine]
@@ -145,7 +145,6 @@
         pltpu.make_async_copy(gate_w.at[0], gate_all.at[:, pl.ds(0, units)], local.at[1]),
         pltpu.make_async_copy(up_w.at[0], up_all.at[:, pl.ds(0, units)], local.at[2]),
         pltpu.make_async_copy(down_w.at[0], down_all.at[pl.ds(0, units)], local.at[3]),
-        pltpu.make_async_copy(table, tables.at[0], local.at[4]),
     ]
 
     def start(copies):
@@ -209,9 +208,15 @@
 
     start(direct[0])
     start(to_z[2:] + to_z[1:2])
-    start(table_z[1:])
     start(weights)
     start(loads)
+    shares = scores[...] / jnp.sum(scores[...], axis=0, keepdims=True)
+    number = lax.broadcasted_iota(jnp.int32, (16, n_rows), 0)
+    table = jnp.zeros((16, n_rows), jnp.float32)
+    for k in range(ids.shape[0]):
+        table = table + jnp.where(ids[k : k + 1, :] == number, shares[k : k + 1, :], 0.0)
+    tables[0] = table
+    start(table_z[1:])
     pass_on(0)
     spread(2)
     for copy in loads:
@@ -222,16 +227,16 @@
     spread(3)
     answer(2, True)
     pass_on(3)
-    answer(3, True)
+    answer(1, True)
     join(2)
     start(ahead[0] + plain[0])
-    answer(1, True)
+    answer(3, True)
+    join(1)
+    go_home(2)
     join(3)
-    go_home(2)
-    join(1)
+    go_home(1)
+    join(0)
     go_home(3)
-    join(0)
-    go_home(1)
     total = gathered(0)
     arrive(to_home[1:])
     for j in (1, 2, 3):
@@ -248,14 +253,13 @@
     n_rows, cols = tokens.shape
     _, width, units = w_gate.shape
     half = n_rows // 2
-    shares = router_scores / jnp.sum(router_scores, axis=1, keepdims=True)
-    number = jnp.arange(16, dtype=jnp.int32)[:, None, None]
-    table = jnp.sum(jnp.where(expert_ids.T[None] == number, shares.T[None], 0.0), axis=1)
     bf16 = jnp.bfloat16
     return pl.pallas_call(
         dense_kernel,
         out_shape=jax.ShapeDtypeStruct((n_rows, cols), bf16),
-        in_specs=[pl.BlockSpec(memory_space=pltpu.HBM)] * 5,
+        in_specs=[pl.BlockSpec(memory_space=pltpu.HBM)]
+        + [pl.BlockSpec(memory_space=pltpu.VMEM)] * 2
+        + [pl.BlockSpec(memory_space=pltpu.HBM)] * 3,
         out_specs=pl.BlockSpec(memory_space=pltpu.VMEM),
         scratch_shapes=[
             pltpu.VMEM((4, n_rows, width), bf16),
@@ -272,7 +276,7 @@
             pltpu.VMEM((4, n_rows, cols), bf16),
             pltpu.SemaphoreType.DMA((55,)),
             pltpu.SemaphoreType.DMA((55,)),
-            pltpu.SemaphoreType.DMA((5,)),
+            pltpu.SemaphoreType.DMA((4,)),
         ],
         compiler_params=pltpu.CompilerParams(
             collective_id=0, has_side_effects=True, vmem_limit_bytes=62 * 1024 * 1024
@@ -282,7 +286,7 @@
             bytes_accessed=6 * width * units * 2,
             transcendentals=4 * n_rows * 2 * units,
         ),
-    )(tokens, table, w_gate, w_up, w_down)
+    )(tokens, expert_ids.T, router_scores.T, w_gate, w_up, w_down)
 
 
 def pick_body(tokens, expert_ids, router_scores, w_gate, w_up, w_down):

time: 96.4 us -> 90.9 us (0.943)
  Pallas kernels: 91.7 us -> 88.7 us
  other arithmetic: 2.76 us -> 0 us
    pallas_call x1, Pallas kernels: 91.7 us -> 88.7 us  [dense_body(): pl.pallas_call(dense_kernel, out_shape=jax.ShapeDtypeStruct((n_rows, cols...]
    reduce_sum x2 -> x0, other arithmetic: 2.06 us -> none  [the longest x1 1.35 us: dense_body(): jnp.sum(jnp.where(expert_ids.T[None] == number, shares.T[None], 0.0), axi...]
where the time goes in v4:
time: 90.9 us; the launch traced here: 90.4 us
  Pallas kernels  88.7 us (98%)
  local copies, waits for them, and re-layouts  1.67 us (2%)
    pallas_call x1, Pallas kernels, dense_body(): pl.pallas_call(dense_kernel, out_shape=jax.ShapeDtypeStruct((n_rows, cols...  88.7 us

profile of v4, /device:TPU:0, one launch (start us, length us, event | category | flops | bytes accessed | tf_op | source)
XLA Modules:
  0.0 90.4 jit_solution(16570600114240525488)
XLA Ops:
  0.0 88.7 %shard_map.64 = bf16[256,512]{1,0:T(8,128)(2,1)} custom-call(bf16[256,512]{1,0:T(8,128)(2,1)} %tokens.1, s32[8,256]{1,0:T(8,128)} %bitcast.2, f32[8,256]{1,0:T(8,128)} %bitcast.3, bf16[1,2048,384]{2,1,0:T(8,128)(2,1)} %gate_w.1, bf16[1,2048,384]{2,1,0:T(8,128)(2,1)} %up_w.1, bf16[1,384,2048]{2,1,0:T(8,128)(2,1)} %down_w.1), custom_call_target="tpu_custom_call" | custom-call | flops 9663676416 | bytes 9437184 | tf_op jit(solution)/shard_map/pallas_call | solution.py:257
  88.7 1.7 %copy.8 = bf16[256,512]{1,0:T(8,128)(2,1)} copy(bf16[256,512]{1,0:T(8,128)(2,1)} %shard_map.64) | data formatting | bytes 524288
